TPU v7x, 512 devices: a whole 4x8x8 slice. The times are simulated.
512 devices in a mesh: grp: 8 (over y), sub: 64 (over z, x, core).
Axes of the slice: x: 4, y: 8, z: 8, core: 2. Of those that a mesh axis runs over, the one named last changes fastest.
Arguments:
- right_sides: float32 [262144, 128], P(('grp', 'sub')), may hold values from -6 to 6
- basis_u: bfloat16 [5, 262144, 256], P(None, ('grp', 'sub')), may hold values from -0.15625 to 0.15625
- basis_v: bfloat16 [5, 262144, 256], P(None, ('grp', 'sub')), may hold values from -0.25 to 0.25
- coupling: bfloat16 [5, 131072, 512], P(None, ('grp', 'sub')), may hold values from -0.03314563 to 0.03314563, as said below
Outputs:
- solution: float32 [262144, 128], P(('grp', 'sub'))
Inputs may be any that keep to these rules, and one draw needn't show every extreme that they name: For level l the 256 rows of coupling on a device equal those on every device whose index (grp major) agrees with it in all bits from bit 9 - 5 + l upwards. Entries of level l are independent, of mean 0 and deviation (2 * 256 * 2**(4 + l))**-0.5, and lie within three such deviations.
All inputs are finite; a program needn't handle non-finite values.
Results may differ from a plain program's by a relative error of at most 0.0003.
Values sent between devices are 32-bit elements; how exact they have to be, the bound alone decides.
A program may use at most 64 MiB of HBM per device.

v0:
```python
import jax
import jax.numpy as jnp
from jax import lax
from jax.sharding import PartitionSpec as P


def swapped(value, axis, bit):
    mask = 2**bit
    pairs = [(source, source ^ mask) for source in range(lax.axis_size(axis))]
    return lax.ppermute(value, axis, pairs)


def partner(value, bit, sub_bits):
    if bit < sub_bits:
        return swapped(value, "sub", bit)
    return swapped(value, "grp", bit - sub_bits)


def pairwise(own_sum, first_bit, span_bits, sub_bits, lower_half):
    for bit in range(first_bit, span_bits):
        own_sum = own_sum + partner(own_sum, bit, sub_bits)
    other_sum = partner(own_sum, span_bits, sub_bits)
    first_half = jnp.where(lower_half, own_sum, other_sum)
    second_half = jnp.where(lower_half, other_sum, own_sum)
    return jnp.concatenate([first_half, second_half], axis=0)


def per_device(right_sides, basis_u, basis_v, coupling):
    highest = lax.Precision.HIGHEST
    sub_bits = lax.axis_size("sub").bit_length() - 1
    all_bits = sub_bits + lax.axis_size("grp").bit_length() - 1
    levels = basis_u.shape[0]
    position = lax.axis_index("grp") * lax.axis_size("sub") + lax.axis_index("sub")
    current = right_sides
    for height in range(levels):
        span_bits = all_bits - levels + height
        v_basis = basis_v[height].astype(jnp.float32)
        own_sum = jnp.einsum("pr,pn->rn", v_basis, current, precision=highest)
        lower_half = jnp.bitwise_and(jnp.right_shift(position, span_bits), 1) == 0
        node_sum = pairwise(own_sum, 0, span_bits, sub_bits, lower_half)
        weights = jnp.dot(coupling[height].astype(jnp.float32), node_sum, precision=highest)
        current = current - jnp.dot(basis_u[height].astype(jnp.float32), weights, precision=highest)
    return current


def solution(mesh):
    in_specs = (
        P(("grp", "sub"), None),
        P(None, ("grp", "sub"), None),
        P(None, ("grp", "sub"), None),
        P(None, ("grp", "sub"), None),
    )
    out_specs = P(("grp", "sub"), None)
    return jax.shard_map(
        per_device, mesh=mesh, in_specs=in_specs, out_specs=out_specs, check_vma=False
    )
```

profile of v0, /device:TPU:194, one launch (start us, length us, event | category | flops | bytes accessed | tf_op | source)
XLA Modules:
  0.0 292.1 jit_solution(16029133345947577586)
XLA Ops:
  7.2 5.0 %collective-permute-done.1 = f32[256,128]{1,0:T(8,128)S(1)} collective-permute-done((f32[256,128]{1,0:T(8,128)S(1)}, f32[256,128]{1,0:T(8,128)S(1)}, u32[]{:S(2)}, u32[]{:S(2)}) %collective-permute-start.1) | collective-permute-done | bytes 131104 | tf_op jit(solution)/shard_map/ppermute | solution.py:10
  30.4 5.9 %collective-permute-done.4 = f32[256,128]{1,0:T(8,128)S(1)} collective-permute-done((f32[256,128]{1,0:T(8,128)S(1)}, f32[256,128]{1,0:T(8,128)S(1)}, u32[]{:S(2)}, u32[]{:S(2)}) %collective-permute-start.4) | collective-permute-done | bytes 131104 | tf_op jit(solution)/shard_map/ppermute | solution.py:10
  66.9 6.1 %collective-permute-done.9 = f32[256,128]{0,1:T(8,128)S(1)} collective-permute-done((f32[256,128]{0,1:T(8,128)S(1)}, f32[256,128]{0,1:T(8,128)S(1)}, u32[]{:S(2)}, u32[]{:S(2)}) %collective-permute-start.9) | collective-permute-done | bytes 131104 | tf_op jit(solution)/shard_map/ppermute | solution.py:10
  73.0 10.3 %collective-permute-start.10 = (f32[256,128]{0,1:T(8,128)S(1)}, f32[256,128]{0,1:T(8,128)S(1)}, u32[]{:S(2)}, u32[]{:S(2)}) collective-permute-start(f32[256,128]{0,1:T(8,128)S(1)} %add.102), channel_id=1, source_target_pairs={{0,32},{1,33},{2,34},{3,35},{4,36},{5,37},{6,38},{7,39},{8,40},{9,... | collective-permute-start | bytes 393224 | tf_op jit(solution)/shard_map/ppermute | solution.py:10
  94.8 5.5 %collective-permute-done.12 = f32[256,128]{0,1:T(8,128)S(1)} collective-permute-done((f32[256,128]{0,1:T(8,128)S(1)}, f32[256,128]{0,1:T(8,128)S(1)}, u32[]{:S(2)}, u32[]{:S(2)}) %collective-permute-start.12) | collective-permute-done | bytes 131104 | tf_op jit(solution)/shard_map/ppermute | solution.py:10
  103.0 5.7 %collective-permute-done.13 = f32[256,128]{0,1:T(8,128)S(1)} collective-permute-done((f32[256,128]{0,1:T(8,128)S(1)}, f32[256,128]{0,1:T(8,128)S(1)}, u32[]{:S(2)}, u32[]{:S(2)}) %collective-permute-start.13) | collective-permute-done | bytes 131104 | tf_op jit(solution)/shard_map/ppermute | solution.py:10
  117.6 6.7 %collective-permute-done.15 = f32[256,128]{0,1:T(8,128)S(1)} collective-permute-done((f32[256,128]{0,1:T(8,128)S(1)}, f32[256,128]{0,1:T(8,128)S(1)}, u32[]{:S(2)}, u32[]{:S(2)}) %collective-permute-start.15) | collective-permute-done | bytes 131104 | tf_op jit(solution)/shard_map/ppermute | solution.py:10
  124.3 6.5 %collective-permute-start.16 = (f32[256,128]{0,1:T(8,128)S(1)}, f32[256,128]{0,1:T(8,128)S(1)}, u32[]{:S(2)}, u32[]{:S(2)}) collective-permute-start(f32[256,128]{0,1:T(8,128)S(1)} %add.107), channel_id=1, source_target_pairs={{0,32},{1,33},{2,34},{3,35},{4,36},{5,37},{6,38},{7,39},{8,40},{9,... | collective-permute-start | bytes 393224 | tf_op jit(solution)/shard_map/ppermute | solution.py:10
  130.8 5.7 %collective-permute-done.16 = f32[256,128]{0,1:T(8,128)S(1)} collective-permute-done((f32[256,128]{0,1:T(8,128)S(1)}, f32[256,128]{0,1:T(8,128)S(1)}, u32[]{:S(2)}, u32[]{:S(2)}) %collective-permute-start.16) | collective-permute-done | bytes 131104 | tf_op jit(solution)/shard_map/ppermute | solution.py:10
  150.9 5.2 %collective-permute-done.19 = f32[256,128]{0,1:T(8,128)S(1)} collective-permute-done((f32[256,128]{0,1:T(8,128)S(1)}, f32[256,128]{0,1:T(8,128)S(1)}, u32[]{:S(2)}, u32[]{:S(2)}) %collective-permute-start.19) | collective-permute-done | bytes 131104 | tf_op jit(solution)/shard_map/ppermute | solution.py:10
  158.9 5.6 %collective-permute-done.20 = f32[256,128]{0,1:T(8,128)S(1)} collective-permute-done((f32[256,128]{0,1:T(8,128)S(1)}, f32[256,128]{0,1:T(8,128)S(1)}, u32[]{:S(2)}, u32[]{:S(2)}) %collective-permute-start.20) | collective-permute-done | bytes 131104 | tf_op jit(solution)/shard_map/ppermute | solution.py:10
  173.3 6.7 %collective-permute-done.22 = f32[256,128]{0,1:T(8,128)S(1)} collective-permute-done((f32[256,128]{0,1:T(8,128)S(1)}, f32[256,128]{0,1:T(8,128)S(1)}, u32[]{:S(2)}, u32[]{:S(2)}) %collective-permute-start.22) | collective-permute-done | bytes 131104 | tf_op jit(solution)/shard_map/ppermute | solution.py:10
  180.0 6.1 %collective-permute-start.23 = (f32[256,128]{0,1:T(8,128)S(1)}, f32[256,128]{0,1:T(8,128)S(1)}, u32[]{:S(2)}, u32[]{:S(2)}) collective-permute-start(f32[256,128]{0,1:T(8,128)S(1)} %add.113), channel_id=1, source_target_pairs={{0,32},{1,33},{2,34},{3,35},{4,36},{5,37},{6,38},{7,39},{8,40},{9,... | collective-permute-start | bytes 393224 | tf_op jit(solution)/shard_map/ppermute | solution.py:10
  186.2 6.0 %collective-permute-done.23 = f32[256,128]{0,1:T(8,128)S(1)} collective-permute-done((f32[256,128]{0,1:T(8,128)S(1)}, f32[256,128]{0,1:T(8,128)S(1)}, u32[]{:S(2)}, u32[]{:S(2)}) %collective-permute-start.23) | collective-permute-done | bytes 131104 | tf_op jit(solution)/shard_map/ppermute | solution.py:10
  194.5 5.1 %collective-permute-done.24 = f32[256,128]{0,1:T(8,128)S(1)} collective-permute-done((f32[256,128]{0,1:T(8,128)S(1)}, f32[256,128]{0,1:T(8,128)S(1)}, u32[]{:S(2)}, u32[]{:S(2)}) %collective-permute-start.24) | collective-permute-done | bytes 131104 | tf_op jit(solution)/shard_map/ppermute | solution.py:10
  203.5 5.3 %collective-permute-done.25 = f32[256,128]{0,1:T(8,128)S(1)} collective-permute-done((f32[256,128]{0,1:T(8,128)S(1)}, f32[256,128]{0,1:T(8,128)S(1)}, u32[]{:S(2)}, u32[]{:S(2)}) %collective-permute-start.25) | collective-permute-done | bytes 131104 | tf_op jit(solution)/shard_map/ppermute | solution.py:10
  223.6 6.4 %collective-permute-done.28 = f32[256,128]{0,1:T(8,128)S(1)} collective-permute-done((f32[256,128]{0,1:T(8,128)S(1)}, f32[256,128]{0,1:T(8,128)S(1)}, u32[]{:S(2)}, u32[]{:S(2)}) %collective-permute-start.28) | collective-permute-done | bytes 131104 | tf_op jit(solution)/shard_map/ppermute | solution.py:10
  238.8 6.7 %collective-permute-done.30 = f32[256,128]{0,1:T(8,128)S(1)} collective-permute-done((f32[256,128]{0,1:T(8,128)S(1)}, f32[256,128]{0,1:T(8,128)S(1)}, u32[]{:S(2)}, u32[]{:S(2)}) %collective-permute-start.30) | collective-permute-done | bytes 131104 | tf_op jit(solution)/shard_map/ppermute | solution.py:10
  245.5 5.2 %collective-permute-start.31 = (f32[256,128]{0,1:T(8,128)S(1)}, f32[256,128]{0,1:T(8,128)S(1)}, u32[]{:S(2)}, u32[]{:S(2)}) collective-permute-start(f32[256,128]{0,1:T(8,128)S(1)} %add.120), channel_id=1, source_target_pairs={{0,32},{1,33},{2,34},{3,35},{4,36},{5,37},{6,38},{7,39},{8,40},{9,... | collective-permute-start | bytes 393224 | tf_op jit(solution)/shard_map/ppermute | solution.py:10
  250.8 6.9 %collective-permute-done.31 = f32[256,128]{0,1:T(8,128)S(1)} collective-permute-done((f32[256,128]{0,1:T(8,128)S(1)}, f32[256,128]{0,1:T(8,128)S(1)}, u32[]{:S(2)}, u32[]{:S(2)}) %collective-permute-start.31) | collective-permute-done | bytes 131104 | tf_op jit(solution)/shard_map/ppermute | solution.py:10
  259.6 5.6 %collective-permute-done.32 = f32[256,128]{0,1:T(8,128)S(1)} collective-permute-done((f32[256,128]{0,1:T(8,128)S(1)}, f32[256,128]{0,1:T(8,128)S(1)}, u32[]{:S(2)}, u32[]{:S(2)}) %collective-permute-start.32) | collective-permute-done | bytes 131104 | tf_op jit(solution)/shard_map/ppermute | solution.py:10
  268.4 8.9 %collective-permute-done.33 = f32[256,128]{0,1:T(8,128)S(1)} collective-permute-done((f32[256,128]{0,1:T(8,128)S(1)}, f32[256,128]{0,1:T(8,128)S(1)}, u32[]{:S(2)}, u32[]{:S(2)}) %collective-permute-start.33) | collective-permute-done | bytes 131104 | tf_op jit(solution)/shard_map/ppermute | solution.py:10
  277.3 5.9 %collective-permute-start.34 = (f32[256,128]{0,1:T(8,128)S(1)}, f32[256,128]{0,1:T(8,128)S(1)}, u32[]{:S(2)}, u32[]{:S(2)}) collective-permute-start(f32[256,128]{0,1:T(8,128)S(1)} %add.123), channel_id=1, source_target_pairs={{0,256},{64,320},{128,384},{192,448},{256,0},{320,64},{384,128},{4... | collective-permute-start | bytes 393224 | tf_op jit(solution)/shard_map/ppermute | solution.py:10
  283.2 6.3 %collective-permute-done.34 = f32[256,128]{0,1:T(8,128)S(1)} collective-permute-done((f32[256,128]{0,1:T(8,128)S(1)}, f32[256,128]{0,1:T(8,128)S(1)}, u32[]{:S(2)}, u32[]{:S(2)}) %collective-permute-start.34) | collective-permute-done | bytes 131104 | tf_op jit(solution)/shard_map/ppermute | solution.py:10
  (104 shorter events, 142.2 us)
Async XLA Ops:
  4.8 7.4 %collective-permute-start.1 = (f32[256,128]{1,0:T(8,128)S(1)}, f32[256,128]{1,0:T(8,128)S(1)}, u32[]{:S(2)}, u32[]{:S(2)}) collective-permute-start(f32[256,128]{1,0:T(8,128)S(1)} %add.94), channel_id=1, source_target_pairs={{0,2},{1,3},{2,0},{3,1},{4,6},{5,7},{6,4},{7,5},{8,10},{9,11},{10,... | collective-permute-start | bytes 393224 | tf_op jit(solution)/shard_map/ppermute | solution.py:10
  12.2 8.5 %collective-permute-start.2 = (f32[256,128]{1,0:T(8,128)S(1)}, f32[256,128]{1,0:T(8,128)S(1)}, u32[]{:S(2)}, u32[]{:S(2)}) collective-permute-start(f32[256,128]{1,0:T(8,128)S(1)} %add.95), channel_id=1, source_target_pairs={{0,4},{1,5},{2,6},{3,7},{4,0},{5,1},{6,2},{7,3},{8,12},{9,13},{10,... | collective-permute-start | bytes 393224 | tf_op jit(solution)/shard_map/ppermute | solution.py:10
  27.6 8.6 %collective-permute-start.4 = (f32[256,128]{1,0:T(8,128)S(1)}, f32[256,128]{1,0:T(8,128)S(1)}, u32[]{:S(2)}, u32[]{:S(2)}) collective-permute-start(f32[256,128]{1,0:T(8,128)S(1)} %add.97), channel_id=1, source_target_pairs={{0,16},{1,17},{2,18},{3,19},{4,20},{5,21},{6,22},{7,23},{8,24},{9,... | collective-permute-start | bytes 393224 | tf_op jit(solution)/shard_map/ppermute | solution.py:10
  41.6 7.4 %collective-permute-start.6 = (f32[256,128]{0,1:T(8,128)S(1)}, f32[256,128]{0,1:T(8,128)S(1)}, u32[]{:S(2)}, u32[]{:S(2)}) collective-permute-start(f32[256,128]{0,1:T(8,128)S(1)} %add.98), channel_id=1, source_target_pairs={{0,2},{1,3},{2,0},{3,1},{4,6},{5,7},{6,4},{7,5},{8,10},{9,11},{10,... | collective-permute-start | bytes 393224 | tf_op jit(solution)/shard_map/ppermute | solution.py:10
  49.1 8.4 %collective-permute-start.7 = (f32[256,128]{0,1:T(8,128)S(1)}, f32[256,128]{0,1:T(8,128)S(1)}, u32[]{:S(2)}, u32[]{:S(2)}) collective-permute-start(f32[256,128]{0,1:T(8,128)S(1)} %add.99), channel_id=1, source_target_pairs={{0,4},{1,5},{2,6},{3,7},{4,0},{5,1},{6,2},{7,3},{8,12},{9,13},{10,... | collective-permute-start | bytes 393224 | tf_op jit(solution)/shard_map/ppermute | solution.py:10
  64.3 8.6 %collective-permute-start.9 = (f32[256,128]{0,1:T(8,128)S(1)}, f32[256,128]{0,1:T(8,128)S(1)}, u32[]{:S(2)}, u32[]{:S(2)}) collective-permute-start(f32[256,128]{0,1:T(8,128)S(1)} %add.101), channel_id=1, source_target_pairs={{0,16},{1,17},{2,18},{3,19},{4,20},{5,21},{6,22},{7,23},{8,24},{9,... | collective-permute-start | bytes 393224 | tf_op jit(solution)/shard_map/ppermute | solution.py:10
  73.0 14.6 %collective-permute-start.10 = (f32[256,128]{0,1:T(8,128)S(1)}, f32[256,128]{0,1:T(8,128)S(1)}, u32[]{:S(2)}, u32[]{:S(2)}) collective-permute-start(f32[256,128]{0,1:T(8,128)S(1)} %add.102), channel_id=1, source_target_pairs={{0,32},{1,33},{2,34},{3,35},{4,36},{5,37},{6,38},{7,39},{8,40},{9,... | collective-permute-start | bytes 393224 | tf_op jit(solution)/shard_map/ppermute | solution.py:10
  92.9 7.4 %collective-permute-start.12 = (f32[256,128]{0,1:T(8,128)S(1)}, f32[256,128]{0,1:T(8,128)S(1)}, u32[]{:S(2)}, u32[]{:S(2)}) collective-permute-start(f32[256,128]{0,1:T(8,128)S(1)} %add.103), channel_id=1, source_target_pairs={{0,2},{1,3},{2,0},{3,1},{4,6},{5,7},{6,4},{7,5},{8,10},{9,11},{10,... | collective-permute-start | bytes 393224 | tf_op jit(solution)/shard_map/ppermute | solution.py:10
  100.4 8.4 %collective-permute-start.13 = (f32[256,128]{0,1:T(8,128)S(1)}, f32[256,128]{0,1:T(8,128)S(1)}, u32[]{:S(2)}, u32[]{:S(2)}) collective-permute-start(f32[256,128]{0,1:T(8,128)S(1)} %add.104), channel_id=1, source_target_pairs={{0,4},{1,5},{2,6},{3,7},{4,0},{5,1},{6,2},{7,3},{8,12},{9,13},{10,... | collective-permute-start | bytes 393224 | tf_op jit(solution)/shard_map/ppermute | solution.py:10
  115.6 8.6 %collective-permute-start.15 = (f32[256,128]{0,1:T(8,128)S(1)}, f32[256,128]{0,1:T(8,128)S(1)}, u32[]{:S(2)}, u32[]{:S(2)}) collective-permute-start(f32[256,128]{0,1:T(8,128)S(1)} %add.106), channel_id=1, source_target_pairs={{0,16},{1,17},{2,18},{3,19},{4,20},{5,21},{6,22},{7,23},{8,24},{9,... | collective-permute-start | bytes 393224 | tf_op jit(solution)/shard_map/ppermute | solution.py:10
  124.3 12.2 %collective-permute-start.16 = (f32[256,128]{0,1:T(8,128)S(1)}, f32[256,128]{0,1:T(8,128)S(1)}, u32[]{:S(2)}, u32[]{:S(2)}) collective-permute-start(f32[256,128]{0,1:T(8,128)S(1)} %add.107), channel_id=1, source_target_pairs={{0,32},{1,33},{2,34},{3,35},{4,36},{5,37},{6,38},{7,39},{8,40},{9,... | collective-permute-start | bytes 393224 | tf_op jit(solution)/shard_map/ppermute | solution.py:10
  148.6 7.4 %collective-permute-start.19 = (f32[256,128]{0,1:T(8,128)S(1)}, f32[256,128]{0,1:T(8,128)S(1)}, u32[]{:S(2)}, u32[]{:S(2)}) collective-permute-start(f32[256,128]{0,1:T(8,128)S(1)} %add.109), channel_id=1, source_target_pairs={{0,2},{1,3},{2,0},{3,1},{4,6},{5,7},{6,4},{7,5},{8,10},{9,11},{10,... | collective-permute-start | bytes 393224 | tf_op jit(solution)/shard_map/ppermute | solution.py:10
  156.1 8.4 %collective-permute-start.20 = (f32[256,128]{0,1:T(8,128)S(1)}, f32[256,128]{0,1:T(8,128)S(1)}, u32[]{:S(2)}, u32[]{:S(2)}) collective-permute-start(f32[256,128]{0,1:T(8,128)S(1)} %add.110), channel_id=1, source_target_pairs={{0,4},{1,5},{2,6},{3,7},{4,0},{5,1},{6,2},{7,3},{8,12},{9,13},{10,... | collective-permute-start | bytes 393224 | tf_op jit(solution)/shard_map/ppermute | solution.py:10
  171.4 8.6 %collective-permute-start.22 = (f32[256,128]{0,1:T(8,128)S(1)}, f32[256,128]{0,1:T(8,128)S(1)}, u32[]{:S(2)}, u32[]{:S(2)}) collective-permute-start(f32[256,128]{0,1:T(8,128)S(1)} %add.112), channel_id=1, source_target_pairs={{0,16},{1,17},{2,18},{3,19},{4,20},{5,21},{6,22},{7,23},{8,24},{9,... | collective-permute-start | bytes 393224 | tf_op jit(solution)/shard_map/ppermute | solution.py:10
  180.0 12.2 %collective-permute-start.23 = (f32[256,128]{0,1:T(8,128)S(1)}, f32[256,128]{0,1:T(8,128)S(1)}, u32[]{:S(2)}, u32[]{:S(2)}) collective-permute-start(f32[256,128]{0,1:T(8,128)S(1)} %add.113), channel_id=1, source_target_pairs={{0,32},{1,33},{2,34},{3,35},{4,36},{5,37},{6,38},{7,39},{8,40},{9,... | collective-permute-start | bytes 393224 | tf_op jit(solution)/shard_map/ppermute | solution.py:10
  192.2 7.4 %collective-permute-start.24 = (f32[256,128]{0,1:T(8,128)S(1)}, f32[256,128]{0,1:T(8,128)S(1)}, u32[]{:S(2)}, u32[]{:S(2)}) collective-permute-start(f32[256,128]{0,1:T(8,128)S(1)} %add.114), channel_id=1, source_target_pairs={{0,64},{64,0},{128,192},{192,128},{256,320},{320,256},{384,448},{4... | collective-permute-start | bytes 393224 | tf_op jit(solution)/shard_map/ppermute | solution.py:10
  199.7 9.2 %collective-permute-start.25 = (f32[256,128]{0,1:T(8,128)S(1)}, f32[256,128]{0,1:T(8,128)S(1)}, u32[]{:S(2)}, u32[]{:S(2)}) collective-permute-start(f32[256,128]{0,1:T(8,128)S(1)} %add.115), channel_id=1, source_target_pairs={{0,128},{64,192},{128,0},{192,64},{256,384},{320,448},{384,256},{4... | collective-permute-start | bytes 393224 | tf_op jit(solution)/shard_map/ppermute | solution.py:10
  214.2 7.4 %collective-permute-start.27 = (f32[256,128]{0,1:T(8,128)S(1)}, f32[256,128]{0,1:T(8,128)S(1)}, u32[]{:S(2)}, u32[]{:S(2)}) collective-permute-start(f32[256,128]{0,1:T(8,128)S(1)} %add.116), channel_id=1, source_target_pairs={{0,2},{1,3},{2,0},{3,1},{4,6},{5,7},{6,4},{7,5},{8,10},{9,11},{10,... | collective-permute-start | bytes 393224 | tf_op jit(solution)/shard_map/ppermute | solution.py:10
  221.6 8.4 %collective-permute-start.28 = (f32[256,128]{0,1:T(8,128)S(1)}, f32[256,128]{0,1:T(8,128)S(1)}, u32[]{:S(2)}, u32[]{:S(2)}) collective-permute-start(f32[256,128]{0,1:T(8,128)S(1)} %add.117), channel_id=1, source_target_pairs={{0,4},{1,5},{2,6},{3,7},{4,0},{5,1},{6,2},{7,3},{8,12},{9,13},{10,... | collective-permute-start | bytes 393224 | tf_op jit(solution)/shard_map/ppermute | solution.py:10
  236.9 8.6 %collective-permute-start.30 = (f32[256,128]{0,1:T(8,128)S(1)}, f32[256,128]{0,1:T(8,128)S(1)}, u32[]{:S(2)}, u32[]{:S(2)}) collective-permute-start(f32[256,128]{0,1:T(8,128)S(1)} %add.119), channel_id=1, source_target_pairs={{0,16},{1,17},{2,18},{3,19},{4,20},{5,21},{6,22},{7,23},{8,24},{9,... | collective-permute-start | bytes 393224 | tf_op jit(solution)/shard_map/ppermute | solution.py:10
  245.5 12.2 %collective-permute-start.31 = (f32[256,128]{0,1:T(8,128)S(1)}, f32[256,128]{0,1:T(8,128)S(1)}, u32[]{:S(2)}, u32[]{:S(2)}) collective-permute-start(f32[256,128]{0,1:T(8,128)S(1)} %add.120), channel_id=1, source_target_pairs={{0,32},{1,33},{2,34},{3,35},{4,36},{5,37},{6,38},{7,39},{8,40},{9,... | collective-permute-start | bytes 393224 | tf_op jit(solution)/shard_map/ppermute | solution.py:10
  257.7 7.5 %collective-permute-start.32 = (f32[256,128]{0,1:T(8,128)S(1)}, f32[256,128]{0,1:T(8,128)S(1)}, u32[]{:S(2)}, u32[]{:S(2)}) collective-permute-start(f32[256,128]{0,1:T(8,128)S(1)} %add.121), channel_id=1, source_target_pairs={{0,64},{64,0},{128,192},{192,128},{256,320},{320,256},{384,448},{4... | collective-permute-start | bytes 393224 | tf_op jit(solution)/shard_map/ppermute | solution.py:10
  265.2 12.0 %collective-permute-start.33 = (f32[256,128]{0,1:T(8,128)S(1)}, f32[256,128]{0,1:T(8,128)S(1)}, u32[]{:S(2)}, u32[]{:S(2)}) collective-permute-start(f32[256,128]{0,1:T(8,128)S(1)} %add.122), channel_id=1, source_target_pairs={{0,128},{64,192},{128,0},{192,64},{256,384},{320,448},{384,256},{4... | collective-permute-start | bytes 393224 | tf_op jit(solution)/shard_map/ppermute | solution.py:10
  277.3 12.2 %collective-permute-start.34 = (f32[256,128]{0,1:T(8,128)S(1)}, f32[256,128]{0,1:T(8,128)S(1)}, u32[]{:S(2)}, u32[]{:S(2)}) collective-permute-start(f32[256,128]{0,1:T(8,128)S(1)} %add.123), channel_id=1, source_target_pairs={{0,256},{64,320},{128,384},{192,448},{256,0},{320,64},{384,128},{4... | collective-permute-start | bytes 393224 | tf_op jit(solution)/shard_map/ppermute | solution.py:10
  (14 other events, 120.8 us)
where the time goes:
time: 293 us; the launch traced here: 292 us
  waiting for transfers between devices  173 us (59%)
  starting transfers between devices  105 us (36%)
  matrix products  11.3 us (4%)
    ppermute x35, waiting for transfers between devices, swapped(): return lax.ppermute(value, axis, pairs)  173 us
    ppermute x35, starting transfers between devices, swapped(): return lax.ppermute(value, axis, pairs)  105 us
    dot_general x5, matrix products, per_device(): jnp.dot(coupling[height].astype(jnp.float32), node_sum, precision=highest)  6.74 us
  transfers between devices with their start and end apart: 35, of which 35 were waited for; matrix products, arithmetic and copies ran while one was open for 0% of the time, Pallas kernels for 0%

commit v1 on v0

v1 whole, which is shorter than its diff:
```python
import functools

import jax
import jax.numpy as jnp
from jax import lax
from jax.experimental import pallas as pl
from jax.experimental.pallas import tpu as pltpu
from jax.sharding import PartitionSpec as P

F32 = jnp.float32
BF16 = jnp.bfloat16
RANK = 256
PTS = 512
COLS = 128
LEVELS = 5
SEMS = 224
SL = 8
XS = 16
XA = ((2, 1), (3, 1), (4, 1))
XB = ((3, 2), (4, 2), (4, 3))


def split2(a):
    hi = a.astype(BF16)
    lo = (a - hi.astype(F32)).astype(BF16)
    return hi, lo


def stacked(a):
    hi = a.astype(BF16).astype(F32)
    return jnp.concatenate([hi, a - hi], axis=0).astype(BF16)


def mm(a, b):
    return lax.dot_general(a, b, (((1,), (0,)), ((), ())), preferred_element_type=F32)


def mm_t(a, b):
    return lax.dot_general(a, b, (((1,), (1,)), ((), ())), preferred_element_type=F32)


def halves(a):
    n = a.shape[0] // 2
    return a[:n] + a[n:]


def kernel(rs_hbm, u_hbm, v_hbm, c_hbm, out_ref, r0, u, v, cpl, cur_t,
           l0, rc0, r0s, l1, rc1, r1s, la, rca, ras, lb, rcb, rbs,
           sla, slb, zar, zbr, ybr, xa, xb, xah, xal, xbh, xbl,
           p0, q0r, p1, q1p, q1s, p2, q2p, q2s, p3, q3p, q3s, p4, q4p,
           wown, wall, ld, ss, rs):
    y = lax.axis_index("grp")
    s = lax.axis_index("sub")
    core = s % 2
    chip = (s // 2) % 8
    plane = s // 16
    lane = s % 16
    base = s - lane

    def near(k):
        return (y, base + (lane + k) % 16)

    def same_core(k):
        return (y, base + 2 * ((chip + k) % 8) + core)

    other_core = (y, s + 1 - 2 * core)
    plane_by = {1: plane + 1 - 2 * (plane % 2), 2: (plane + 2) % 4, 3: 3 - plane}
    y2 = y + 2 - 4 * ((y // 2) % 2)
    y_by = {1: y + 1 - 2 * (y % 2), 2: y2, 3: 4 * (y // 4) + 3 - y % 4, 4: (y + 4) % 8, 6: (y2 + 4) % 8}

    def far(zmask, ymask):
        ss_ = s + 16 * (plane_by[zmask] - plane) if zmask else s
        return (y_by[ymask] if ymask else y, ss_)

    far_masks = [(1, 0), (2, 0), (3, 0), (0, 1), (2, 1), (0, 2), (0, 3), (0, 4), (0, 6)]
    MESH = pl.DeviceIdType.MESH
    barrier = pltpu.get_barrier_semaphore()
    for m in far_masks:
        pl.semaphore_signal(barrier, inc=1, device_id=far(*m), device_id_type=MESH)
    for k in range(1, 16):
        pl.semaphore_signal(barrier, inc=1, device_id=near(k), device_id_type=MESH)

    loads = {}

    def load(name, src, dst):
        loads[name] = pltpu.make_async_copy(src, dst, ld.at[len(loads)])
        loads[name].start()

    load("r", rs_hbm, r0)
    load("v0", v_hbm.at[0], v.at[0])
    load("u1", u_hbm.at[1], u.at[1])
    for m in (2, 3, 4):
        load("v%d" % m, v_hbm.at[m], v.at[m])
    load("c0", c_hbm.at[0], cpl.at[0])
    load("u2", u_hbm.at[2], u.at[2])
    load("u3", u_hbm.at[3], u.at[3])
    load("u0", u_hbm.at[0], u.at[0])
    load("v1", v_hbm.at[1], v.at[1])
    for m in (1, 2, 3, 4):
        load("c%d" % m, c_hbm.at[m], cpl.at[m])
    load("u4", u_hbm.at[4], u.at[4])

    pending = []
    count = [0]

    def send(src, dst, device):
        i = count[0]
        count[0] += 1
        cp = pltpu.make_async_remote_copy(src_ref=src, dst_ref=dst, send_sem=ss.at[i], recv_sem=rs.at[i],
                                          device_id=device, device_id_type=MESH)
        cp.start()
        pending.append(cp)
        return cp

    def flush():
        for cp in pending:
            cp.wait_send()
        pending.clear()

    def core_send(l, rc):
        return send(l.at[1 - core], rc, other_core)

    def core_add(cp, l, rc):
        cp.wait_recv()
        rc[...] = rc[...] + l[core]

    def rs_send(rc, slots):
        return [send(rc.at[(chip + k) % 8], slots.at[k - 1], same_core(k)) for k in range(1, 8)]

    def rs_sum(cps, rc, slots):
        for cp in cps:
            cp.wait_recv()
        total = rc[chip]
        for k in range(7):
            total = total + slots[k]
        return total

    def ag_send(src, full, first=None, size=None):
        out = []
        for k in range(1, 8):
            def at(i):
                return full.at[core, i] if first is None else full.at[core, i, pl.ds(first, size)]
            cp = send(src, at(chip), same_core(k))
            arrive = pltpu.make_async_remote_copy(src_ref=src, dst_ref=at((chip + 8 - k) % 8), send_sem=ss.at[count[0] - 1],
                                                  recv_sem=rs.at[count[0] - 1], device_id=same_core(k), device_id_type=MESH)
            out.append(arrive)
        return out

    def share_send(cps, full):
        for cp in cps:
            cp.wait_recv()
        cp = send(full.at[core], full.at[core], other_core)
        return pltpu.make_async_remote_copy(src_ref=full.at[core], dst_ref=full.at[1 - core], send_sem=ss.at[count[0] - 1],
                                            recv_sem=rs.at[count[0] - 1], device_id=other_core, device_id_type=MESH)

    def w_send(level, value):
        wown[level] = value
        wall[level, core * 8 + chip] = value
        out = []
        for k in range(1, 16):
            send(wown.at[level], wall.at[level, core * 8 + chip], near(k))
            frm = (lane + 16 - k) % 16
            i = count[0] - 1
            out.append(pltpu.make_async_remote_copy(
                src_ref=wown.at[level], dst_ref=wall.at[level, (frm % 2) * 8 + frm // 2], send_sem=ss.at[i],
                recv_sem=rs.at[i], device_id=near(k), device_id_type=MESH))
        return out

    def w_full(level, cps):
        for cp in cps:
            cp.wait_recv()
        return stacked(wall[level].reshape(COLS, RANK))

    def weights(level, own, sibling, upper):
        loads["c%d" % level].wait()
        first = jnp.where(upper == 0, own, sibling)
        second = jnp.where(upper == 0, sibling, own)
        node = jnp.concatenate([first, second], axis=1)
        return halves(mm_t(stacked(node), cpl[level]))

    def slices(value, n):
        return value.reshape(2, 8, n, RANK)

    loads["r"].wait()
    rt = r0[...].T
    cur_t[...] = rt
    loads["v0"].wait()
    l0[...] = slices(halves(mm(stacked(rt), v[0])), SL)
    pl.semaphore_wait(barrier, len(far_masks) + 15)
    c_0 = core_send(l0, rc0)
    loads["u1"].wait()
    ut = u[1].T
    for i, m in enumerate((2, 3, 4)):
        loads["v%d" % m].wait()
        la[:, :, i * XS:(i + 1) * XS, :] = slices(mm(ut, v[m]), XS)
    core_add(c_0, l0, rc0)
    g_0 = rs_send(rc0, r0s)
    c_a = core_send(la, rca)
    loads["u2"].wait()
    ut = u[2].T
    for i, m in enumerate((3, 4)):
        lb[:, :, i * XS:(i + 1) * XS, :] = slices(mm(ut, v[m]), XS)
    loads["u3"].wait()
    ut = u[3].T
    lb[:, :, 2 * XS:3 * XS, :] = slices(mm(ut, v[4]), XS)
    c_b = core_send(lb, rcb)

    p0[...] = rs_sum(g_0, rc0, r0s)
    e_0 = send(p0, q0r, far(1, 0))
    core_add(c_a, la, rca)
    g_a = rs_send(rca, ras)
    core_add(c_b, lb, rcb)
    g_b = rs_send(rcb, rbs)
    bit4, bit5 = plane % 2, plane // 2
    e_0.wait_recv()
    w_cps = {}
    w_cps[0] = w_send(0, weights(0, p0[...], q0r[...], bit4))

    sla[...] = rs_sum(g_a, rca, ras)
    z_a = send(sla, zar, far(1, 0))

    loads["u0"].wait()
    w0 = w_full(0, w_cps[0])
    cur = cur_t[...] - halves(mm_t(w0, u[0]))
    cur_s = stacked(cur)
    loads["v1"].wait()
    for m in (1, 2, 3, 4):
        l1[:, :, (m - 1) * SL:m * SL, :] = slices(halves(mm(cur_s, v[m])), SL)
    c_1 = core_send(l1, rc1)
    slb[...] = rs_sum(g_b, rcb, rbs)
    z_b = [send(slb, zbr.at[i], far(i + 1, 0)) for i in range(3)]
    z_a.wait_recv()
    sla_sum = sla[...] + zar[...]
    xa[core, chip] = sla_sum
    a_a = ag_send(xa.at[core, chip], xa)
    core_add(c_1, l1, rc1)
    g_1 = rs_send(rc1, r1s)
    acc = r0[...]
    upd = mm_t(u[0], w0)
    out_ref[...] = acc - (upd[:, :COLS] + upd[:, COLS:])
    flush()
    for cp in z_b:
        cp.wait_recv()
    slb_sum = slb[...] + zbr[0] + (zbr[1] + zbr[2])
    xb[core, chip] = slb_sum
    y_b = send(xb.at[core, chip, pl.ds(2 * XS, XS)], ybr, far(0, 1))
    a_b = ag_send(xb.at[core, chip, pl.ds(0, 2 * XS)], xb, 0, 2 * XS)

    p1[...] = rs_sum(g_1, rc1, r1s)
    e_1 = [send(p1.at[pl.ds(0, SL)], q1p.at[i], far(i + 1, 0)) for i in range(3)]
    e_1s = send(p1.at[pl.ds(SL, 3 * SL)], q1s, far(1, 0))
    s_a = share_send(a_a, xa)
    y_b.wait_recv()
    y_b.wait_send()
    pending.remove(y_b)
    xb[core, chip, pl.ds(2 * XS, XS)] = xb[core, chip, pl.ds(2 * XS, XS)] + ybr[...]
    a_c = ag_send(xb.at[core, chip, pl.ds(2 * XS, XS)], xb, 2 * XS, XS)
    s_a.wait_recv()
    for i in range(3):
        hi, lo = split2(xa[:, :, i * XS:(i + 1) * XS, :].reshape(RANK, RANK))
        xah[i], xal[i] = hi, lo

    def product(w_s, hi, lo):
        return halves(mm(w_s, hi)) + mm(w_s, lo)[:SL]

    for cp in e_1:
        cp.wait_recv()
    w = weights(1, p1[0:SL] + q1p[0], q1p[1] + q1p[2], bit5)
    w_cps[1] = w_send(1, w)
    e_1s.wait_recv()
    ws = stacked(w)
    rest = p1[SL:4 * SL] + q1s[...]
    for i in range(3):
        p2[i * SL:(i + 1) * SL] = rest[i * SL:(i + 1) * SL] - product(ws, xah[i], xal[i])
    peers = [(2, 0), (0, 1), (2, 1)]
    e_2 = [send(p2.at[pl.ds(0, SL)], q2p.at[i], far(*peers[i])) for i in range(3)]
    e_2s = send(p2.at[pl.ds(SL, 2 * SL)], q2s, far(2, 0))
    s_b = share_send(a_b + a_c, xb)
    flush()

    def apply(level):
        ws_ = w_full(level, w_cps[level])
        loads["u%d" % level].wait() if level == 4 else None
        upd_ = mm_t(u[level], ws_)
        out_ref[...] = out_ref[...] - (upd_[:, :COLS] + upd_[:, COLS:])

    apply(1)
    s_b.wait_recv()
    for i in range(3):
        hi, lo = split2(xb[:, :, i * XS:(i + 1) * XS, :].reshape(RANK, RANK))
        xbh[i], xbl[i] = hi, lo

    for cp in e_2:
        cp.wait_recv()
    w = weights(2, p2[0:SL] + q2p[0], q2p[1] + q2p[2], y % 2)
    w_cps[2] = w_send(2, w)
    e_2s.wait_recv()
    ws = stacked(w)
    rest = p2[SL:3 * SL] + q2s[...]
    for i in range(2):
        p3[i * SL:(i + 1) * SL] = rest[i * SL:(i + 1) * SL] - product(ws, xbh[i], xbl[i])
    e_3 = [send(p3.at[pl.ds(0, SL)], q3p.at[i], far(0, i + 1)) for i in range(3)]
    e_3s = send(p3.at[pl.ds(SL, SL)], q3s, far(0, 1))
    flush()
    apply(2)

    for cp in e_3:
        cp.wait_recv()
    w = weights(3, p3[0:SL] + q3p[0], q3p[1] + q3p[2], (y // 2) % 2)
    w_cps[3] = w_send(3, w)
    e_3s.wait_recv()
    p4[...] = p3[SL:2 * SL] + q3s[...] - product(stacked(w), xbh[2], xbl[2])
    ymask = (2, 4, 6)
    e_4 = [send(p4, q4p.at[i], far(0, ymask[i])) for i in range(3)]
    flush()
    apply(3)

    for cp in e_4:
        cp.wait_recv()
    w = weights(4, p4[...] + q4p[0], q4p[1] + q4p[2], y // 4)
    w_cps[4] = w_send(4, w)
    apply(4)
    flush()


def per_device(right_sides, basis_u, basis_v, coupling):
    def vm(*shape, dtype=F32):
        return pltpu.VMEM(shape, dtype)

    scratch = [
        vm(PTS, COLS), vm(LEVELS, PTS, RANK, dtype=BF16), vm(LEVELS, PTS, RANK, dtype=BF16),
        vm(LEVELS, RANK, 2 * RANK, dtype=BF16), vm(COLS, PTS),
    ]
    for n in (SL, 4 * SL, 3 * XS, 3 * XS):
        scratch += [vm(2, 8, n, RANK), vm(8, n, RANK), vm(7, n, RANK)]
    scratch += [
        vm(3 * XS, RANK), vm(3 * XS, RANK), vm(3 * XS, RANK), vm(3, 3 * XS, RANK), vm(XS, RANK),
        vm(2, 8, 3 * XS, RANK), vm(2, 8, 3 * XS, RANK),
    ]
    scratch += [vm(3, RANK, RANK, dtype=BF16)] * 4
    scratch += [
        vm(SL, RANK), vm(SL, RANK),
        vm(4 * SL, RANK), vm(3, SL, RANK), vm(3 * SL, RANK),
        vm(3 * SL, RANK), vm(3, SL, RANK), vm(2 * SL, RANK),
        vm(2 * SL, RANK), vm(3, SL, RANK), vm(SL, RANK),
        vm(SL, RANK), vm(3, SL, RANK),
        vm(LEVELS, SL, RANK), vm(LEVELS, 16, SL, RANK),
        pltpu.SemaphoreType.DMA((16,)), pltpu.SemaphoreType.DMA((SEMS,)), pltpu.SemaphoreType.DMA((SEMS,)),
    ]
    return pl.pallas_call(
        kernel,
        out_shape=jax.ShapeDtypeStruct((PTS, COLS), F32),
        in_specs=[pl.BlockSpec(memory_space=pltpu.HBM)] * 4,
        out_specs=pl.BlockSpec(memory_space=pltpu.VMEM),
        scratch_shapes=scratch,
        compiler_params=pltpu.CompilerParams(collective_id=0, has_side_effects=True, vmem_limit_bytes=48 * 2**20),
        name="hodlr_solve",
    )(right_sides, basis_u, basis_v, coupling)


def solution(mesh):
    in_specs = (
        P(("grp", "sub"), None),
        P(None, ("grp", "sub"), None),
        P(None, ("grp", "sub"), None),
        P(None, ("grp", "sub"), None),
    )
    out_specs = P(("grp", "sub"), None)
    return jax.shard_map(
        per_device, mesh=mesh, in_specs=in_specs, out_specs=out_specs, check_vma=False
    )
```

time: 293 us -> 84.2 us (0.29)
  the two profiles are of different devices: /device:TPU:194 before, /device:TPU:1 now
where the time goes in v1:
time: 84.2 us; the launch traced here: 84 us
  Pallas kernels  78.4 us (93%)
  local copies, waits for them, and re-layouts  5.6 us (7%)
    pallas_call x1, Pallas kernels, per_device(): pl.pallas_call(kernel, out_shape=jax.ShapeDtypeStruct((PTS, COLS), F32),...  78.4 us
    unnamed x9, local copies, waits for them, and re-layouts  5.6 us

profile of v1, /device:TPU:1, one launch (start us, length us, event | category | flops | bytes accessed | tf_op | source)
XLA Modules:
  0.0 84.0 jit_solution(10999988525459591146)
XLA Ops:
  0.0 0.0 copy-start
  0.0 1.3 %copy-done = bf16[5,512,256]{2,1,0:T(8,128)(2,1)S(1)} copy-done((bf16[5,512,256]{2,1,0:T(8,128)(2,1)S(1)}, bf16[5,512,256]{2,1,0:T(8,128)(2,1)}, u32[]{:S(2)}) %copy-start) | copy-done | bytes 1310744
  1.3 0.0 copy-start.1
  1.3 1.3 %copy-done.1 = bf16[5,512,256]{2,1,0:T(8,128)(2,1)S(1)} copy-done((bf16[5,512,256]{2,1,0:T(8,128)(2,1)S(1)}, bf16[5,512,256]{2,1,0:T(8,128)(2,1)}, u32[]{:S(2)}) %copy-start.1) | copy-done | bytes 1310744
  2.6 0.0 copy-start.2
  2.6 1.3 %copy-done.2 = bf16[5,256,512]{2,1,0:T(8,128)(2,1)S(1)} copy-done((bf16[5,256,512]{2,1,0:T(8,128)(2,1)S(1)}, bf16[5,256,512]{2,1,0:T(8,128)(2,1)}, u32[]{:S(2)}) %copy-start.2) | copy-done | bytes 1310744
  4.0 0.0 copy-start.3
  4.0 0.9 %copy-done.3 = f32[512,128]{1,0:T(8,128)S(1)} copy-done((f32[512,128]{1,0:T(8,128)S(1)}, f32[512,128]{1,0:T(8,128)}, u32[]{:S(2)}) %copy-start.3) | copy-done | bytes 262168
  4.9 78.4 %hodlr_solve.1 = f32[512,128]{1,0:T(8,128)S(1)} custom-call(f32[512,128]{1,0:T(8,128)S(1)} %copy-done.3, bf16[5,512,256]{2,1,0:T(8,128)(2,1)S(1)} %copy-done, bf16[5,512,256]{2,1,0:T(8,128)(2,1)S(1)} %copy-done.1, bf16[5,256,512]{2,1,0:T(8,128)(2,1)S(1)} %copy-done.2), custom_call_target="tpu_custom_call" | custom-call | tf_op jit(solution)/shard_map/hodlr_solve/pallas_call | solution.py:350
  83.3 0.7 copy.6
Async XLA Ops:
  0.0 1.3 %copy-start = (bf16[5,512,256]{2,1,0:T(8,128)(2,1)S(1)}, bf16[5,512,256]{2,1,0:T(8,128)(2,1)}, u32[]{:S(2)}) copy-start(bf16[5,512,256]{2,1,0:T(8,128)(2,1)} %u_hbm.1) | copy-start | bytes 3932164
  1.3 1.3 %copy-start.1 = (bf16[5,512,256]{2,1,0:T(8,128)(2,1)S(1)}, bf16[5,512,256]{2,1,0:T(8,128)(2,1)}, u32[]{:S(2)}) copy-start(bf16[5,512,256]{2,1,0:T(8,128)(2,1)} %v_hbm.1) | copy-start | bytes 3932164
  2.6 1.3 %copy-start.2 = (bf16[5,256,512]{2,1,0:T(8,128)(2,1)S(1)}, bf16[5,256,512]{2,1,0:T(8,128)(2,1)}, u32[]{:S(2)}) copy-start(bf16[5,256,512]{2,1,0:T(8,128)(2,1)} %c_hbm.1) | copy-start | bytes 3932164
  4.0 0.9 %copy-start.3 = (f32[512,128]{1,0:T(8,128)S(1)}, f32[512,128]{1,0:T(8,128)}, u32[]{:S(2)}) copy-start(f32[512,128]{1,0:T(8,128)} %rs_hbm.1) | copy-start | bytes 786436

commit v2 on v0

v2 whole, which is shorter than its diff:
```python
import functools

import jax
import jax.numpy as jnp
from jax import lax
from jax.experimental import pallas as pl
from jax.experimental.pallas import tpu as pltpu
from jax.sharding import PartitionSpec as P

F32 = jnp.float32
BF16 = jnp.bfloat16
RANK = 256
PTS = 512
COLS = 128
LEVELS = 5
SEMS = 32
SL = 8
XS = 16


def split2(a):
    hi = a.astype(BF16)
    lo = (a - hi.astype(F32)).astype(BF16)
    return hi, lo


def stacked(a):
    hi = a.astype(BF16).astype(F32)
    return jnp.concatenate([hi, a - hi], axis=0).astype(BF16)


def mm(a, b):
    return lax.dot_general(a, b, (((1,), (0,)), ((), ())), preferred_element_type=F32)


def mm_t(a, b):
    return lax.dot_general(a, b, (((1,), (1,)), ((), ())), preferred_element_type=F32)


def halves(a):
    n = a.shape[0] // 2
    return a[:n] + a[n:]


def kernel(rs_hbm, u_hbm, v_hbm, c_hbm, out_ref, r0, u, v, cpl, cur_t,
           l0, rc0, r0s, lx, rcx, rxs, l1, rc1, r1s, lb, rcb, rbs,
           px, slb, zbr, ybr, x1, xb, x1h, x1l, xbh, xbl,
           p0, q0r, p1, q1p, p2, q2p, q2s, p3, q3p, q3s, p4, q4p,
           wall, ld, ss, rs):
    y = lax.axis_index("grp")
    s = lax.axis_index("sub")
    core = s % 2
    chip = (s // 2) % 8
    plane = s // 16
    lane = s % 16
    base = s - lane

    def near(k):
        return (y, base + (lane + k) % 16)

    def same_core(k):
        return (y, base + 2 * ((chip + k) % 8) + core)

    other_core = (y, s + 1 - 2 * core)
    plane_by = {1: plane + 1 - 2 * (plane % 2), 2: (plane + 2) % 4, 3: 3 - plane}
    y2 = y + 2 - 4 * ((y // 2) % 2)
    y_by = {1: y + 1 - 2 * (y % 2), 2: y2, 3: 4 * (y // 4) + 3 - y % 4, 4: (y + 4) % 8, 6: (y2 + 4) % 8}

    def far(zmask, ymask):
        ss_ = s + 16 * (plane_by[zmask] - plane) if zmask else s
        return (y_by[ymask] if ymask else y, ss_)

    far_masks = [(1, 0), (2, 0), (3, 0), (0, 1), (1, 1), (2, 1), (3, 1), (0, 2), (0, 3), (0, 4), (0, 6)]
    MESH = pl.DeviceIdType.MESH
    barrier = pltpu.get_barrier_semaphore()
    for m in far_masks:
        pl.semaphore_signal(barrier, inc=1, device_id=far(*m), device_id_type=MESH)
    for k in range(1, 16):
        pl.semaphore_signal(barrier, inc=1, device_id=near(k), device_id_type=MESH)

    loads = {}

    def load(name, src, dst):
        loads[name] = pltpu.make_async_copy(src, dst, ld.at[len(loads)])
        loads[name].start()

    load("r", rs_hbm, r0)
    for name in ("v0", "u0", "v1", "c0", "u2", "v3", "v4", "u3", "c1", "u1", "v2", "c2", "c3", "c4", "u4"):
        src, dst = {"u": (u_hbm, u), "v": (v_hbm, v), "c": (c_hbm, cpl)}[name[0]]
        load(name, src.at[int(name[1])], dst.at[int(name[1])])

    pending = []
    count = [0]

    def send(copies, total):
        i = count[0]
        count[0] += 1

        def copy(src, dst, device):
            return pltpu.make_async_remote_copy(src_ref=src, dst_ref=dst, send_sem=ss.at[i], recv_sem=rs.at[i],
                                                device_id=device, device_id_type=MESH)

        for one in copies:
            copy(*one).start()
        cp = copy(total, total, copies[0][2])
        pending.append(cp)
        return cp

    def flush():
        for cp in old + pending:
            cp.wait_send()

    old = []

    def flush_old():
        for cp in old:
            cp.wait_send()
        old[:] = pending
        pending.clear()

    def core_send(l, rc):
        return send([(l.at[1 - core], rc, other_core)], rc)

    def core_add(cp, l, rc):
        cp.wait_recv()
        rc[...] = rc[...] + l[core]

    def rs_send(rc, slots):
        return send([(rc.at[(chip + k) % 8], slots.at[k - 1], same_core(k)) for k in range(1, 8)], slots)

    def rs_sum(cp, rc, slots):
        cp.wait_recv()
        total = rc[chip]
        for k in range(7):
            total = total + slots[k]
        return total

    def ag_send(full, first=0, size=XS):
        own = full.at[core, chip, pl.ds(first, size)]
        return send([(own, own, same_core(k)) for k in range(1, 8)], full.at[core, pl.ds(0, 7), pl.ds(first, size)])

    def share_send(cp, full, first=0, size=XS):
        cp.wait_recv()
        rows = pl.ds(first, size)
        return send([(full.at[core, i, rows], full.at[core, i, rows], other_core) for i in range(8)],
                    full.at[1 - core, pl.ds(0, 8), rows])

    def all_send(src, slots, masks):
        return send([(src, slots.at[i], far(*m)) for i, m in enumerate(masks)], slots)

    def w_send(level, value):
        mine = wall.at[level, core * 8 + chip]
        mine[...] = value
        return send([(mine, mine, near(k)) for k in range(1, 16)], wall.at[level, pl.ds(0, 15)])

    def w_full(level, cp):
        cp.wait_recv()
        return stacked(wall[level].reshape(COLS, RANK))

    def weights(level, own, sibling, upper):
        loads["c%d" % level].wait()
        first = jnp.where(upper == 0, own, sibling)
        second = jnp.where(upper == 0, sibling, own)
        node = jnp.concatenate([first, second], axis=1)
        return halves(mm_t(stacked(node), cpl[level]))

    def slices(value, n):
        return value.reshape(2, 8, n, RANK)

    def product(w_s, hi, lo):
        return halves(mm(w_s, hi)) + mm(w_s, lo)[:SL]

    def split_full(full, his, los, first, last):
        for i in range(first, last):
            hi, lo = split2(full[:, :, i * XS:(i + 1) * XS, :].reshape(RANK, RANK))
            his[i], los[i] = hi, lo

    bit4, bit5 = plane % 2, plane // 2
    planes = [(1, 0), (2, 0), (3, 0)]
    w_cps = {}

    loads["r"].wait()
    rt = r0[...].T
    cur_t[...] = rt
    rts = stacked(rt)
    loads["v0"].wait()
    l0[...] = slices(halves(mm(rts, v[0])), SL)
    pl.semaphore_wait(barrier, len(far_masks) + 15)
    c_0 = core_send(l0, rc0)
    loads["v1"].wait()
    loads["u0"].wait()
    lx[:, :, 0:SL, :] = slices(halves(mm(rts, v[1])), SL)
    lx[:, :, SL:SL + XS, :] = slices(mm(u[0].T, v[1]), XS)
    c_x = core_send(lx, rcx)
    core_add(c_0, l0, rc0)
    g_0 = rs_send(rc0, r0s)
    core_add(c_x, lx, rcx)
    g_x = rs_send(rcx, rxs)
    loads["u2"].wait()
    loads["v3"].wait()
    loads["v4"].wait()
    ut = u[2].T
    for i, m in enumerate((3, 4)):
        lb[:, :, i * XS:(i + 1) * XS, :] = slices(mm(ut, v[m]), XS)
    loads["u3"].wait()
    ut = u[3].T
    lb[:, :, 2 * XS:3 * XS, :] = slices(mm(ut, v[4]), XS)
    c_b = core_send(lb, rcb)
    p0[...] = rs_sum(g_0, rc0, r0s)
    e_0 = all_send(p0, q0r, [(1, 0)])
    px[...] = rs_sum(g_x, rcx, rxs)
    x1[core, chip] = px[SL:SL + XS]
    a_x = ag_send(x1)
    core_add(c_b, lb, rcb)
    e_0.wait_recv()
    w_0 = weights(0, p0[...], q0r[0], bit4)
    ws = stacked(w_0)
    w_cps[0] = w_send(0, w_0)
    g_b = rs_send(rcb, rbs)
    s_x = share_send(a_x, x1)
    s_x.wait_recv()
    split_full(x1, x1h, x1l, 0, 1)
    p1[...] = px[0:SL] - product(ws, x1h[0], x1l[0])
    e_1 = all_send(p1, q1p, planes)
    w0 = w_full(0, w_cps[0])
    cur_t[...] = cur_t[...] - halves(mm_t(w0, u[0]))
    upd = mm_t(u[0], w0)
    out_ref[...] = r0[...] - (upd[:, :COLS] + upd[:, COLS:])

    def apply(level, ws_=None):
        if ws_ is None:
            ws_ = w_full(level, w_cps[level])
        if level == 4:
            loads["u4"].wait()
        upd_ = mm_t(u[level], ws_)
        out_ref[...] = out_ref[...] - (upd_[:, :COLS] + upd_[:, COLS:])

    slb[...] = rs_sum(g_b, rcb, rbs)
    z_b = all_send(slb, zbr, planes)

    e_1.wait_recv()
    w_cps[1] = w_send(1, weights(1, p1[...] + q1p[0], q1p[1] + q1p[2], bit5))

    loads["u1"].wait()
    loads["v2"].wait()
    w1 = w_full(1, w_cps[1])
    cur_s = stacked(cur_t[...] - halves(mm_t(w1, u[1])))
    for m in (2, 3, 4):
        l1[:, :, (m - 2) * SL:(m - 1) * SL, :] = slices(halves(mm(cur_s, v[m])), SL)
    c_1 = core_send(l1, rc1)
    core_add(c_1, l1, rc1)
    g_1 = rs_send(rc1, r1s)
    z_b.wait_recv()
    xb[core, chip] = slb[...] + zbr[0] + (zbr[1] + zbr[2])
    y_b = all_send(xb.at[core, chip, pl.ds(2 * XS, XS)], ybr, [(0, 1)])
    a_b = ag_send(xb, 0, 2 * XS)
    p2[...] = rs_sum(g_1, rc1, r1s)
    peers = [(1, 0), (2, 0), (3, 0), (0, 1), (1, 1), (2, 1), (3, 1)]
    e_2 = all_send(p2.at[pl.ds(0, SL)], q2p, peers)
    e_2s = all_send(p2.at[pl.ds(SL, 2 * SL)], q2s, planes)
    flush_old()
    y_b.wait_recv()
    y_b.wait_send()
    old[:] = [cp for cp in old if cp is not y_b]
    xb[core, chip, pl.ds(2 * XS, XS)] = xb[core, chip, pl.ds(2 * XS, XS)] + ybr[0]
    a_c = ag_send(xb, 2 * XS, XS)
    s_b = share_send(a_b, xb, 0, 2 * XS)
    apply(1, w1)

    e_2.wait_recv()
    w = weights(2, (p2[0:SL] + q2p[0]) + (q2p[1] + q2p[2]), (q2p[3] + q2p[4]) + (q2p[5] + q2p[6]), y % 2)
    e_2s.wait_recv()
    rest = (p2[SL:3 * SL] + q2s[0]) + (q2s[1] + q2s[2])
    s_b.wait_recv()
    split_full(xb, xbh, xbl, 0, 2)
    ws = stacked(w)
    for i in range(2):
        p3[i * SL:(i + 1) * SL] = rest[i * SL:(i + 1) * SL] - product(ws, xbh[i], xbl[i])
    e_3 = all_send(p3.at[pl.ds(0, SL)], q3p, [(0, 1), (0, 2), (0, 3)])
    e_3s = all_send(p3.at[pl.ds(SL, SL)], q3s, [(0, 1)])
    w_cps[2] = w_send(2, w)
    flush_old()
    s_c = share_send(a_c, xb, 2 * XS, XS)
    apply(2)
    s_c.wait_recv()
    split_full(xb, xbh, xbl, 2, 3)

    e_3.wait_recv()
    w = weights(3, p3[0:SL] + q3p[0], q3p[1] + q3p[2], (y // 2) % 2)
    e_3s.wait_recv()
    p4[...] = p3[SL:2 * SL] + q3s[0] - product(stacked(w), xbh[2], xbl[2])
    e_4 = all_send(p4, q4p, [(0, 2), (0, 4), (0, 6)])
    flush_old()
    w_cps[3] = w_send(3, w)
    apply(3)

    e_4.wait_recv()
    w = weights(4, p4[...] + q4p[0], q4p[1] + q4p[2], y // 4)
    w_cps[4] = w_send(4, w)
    apply(4)
    flush()


def per_device(right_sides, basis_u, basis_v, coupling):
    def vm(*shape, dtype=F32):
        return pltpu.VMEM(shape, dtype)

    scratch = [
        vm(PTS, COLS), vm(LEVELS, PTS, RANK, dtype=BF16), vm(LEVELS, PTS, RANK, dtype=BF16),
        vm(LEVELS, RANK, 2 * RANK, dtype=BF16), vm(COLS, PTS),
    ]
    for n in (SL, SL + XS, 3 * SL, 3 * XS):
        scratch += [vm(2, 8, n, RANK), vm(8, n, RANK), vm(7, n, RANK)]
    scratch += [
        vm(SL + XS, RANK), vm(3 * XS, RANK), vm(3, 3 * XS, RANK), vm(1, XS, RANK),
        vm(2, 8, XS, RANK), vm(2, 8, 3 * XS, RANK),
    ]
    scratch += [vm(1, RANK, RANK, dtype=BF16)] * 2 + [vm(3, RANK, RANK, dtype=BF16)] * 2
    scratch += [
        vm(SL, RANK), vm(1, SL, RANK),
        vm(SL, RANK), vm(3, SL, RANK),
        vm(3 * SL, RANK), vm(7, SL, RANK), vm(3, 2 * SL, RANK),
        vm(2 * SL, RANK), vm(3, SL, RANK), vm(1, SL, RANK),
        vm(SL, RANK), vm(3, SL, RANK),
        vm(LEVELS, 16, SL, RANK),
        pltpu.SemaphoreType.DMA((16,)), pltpu.SemaphoreType.DMA((SEMS,)), pltpu.SemaphoreType.DMA((SEMS,)),
    ]
    return pl.pallas_call(
        kernel,
        out_shape=jax.ShapeDtypeStruct((PTS, COLS), F32),
        in_specs=[pl.BlockSpec(memory_space=pltpu.HBM)] * 4,
        out_specs=pl.BlockSpec(memory_space=pltpu.VMEM),
        scratch_shapes=scratch,
        compiler_params=pltpu.CompilerParams(collective_id=0, has_side_effects=True, vmem_limit_bytes=60 * 2**20),
        name="hodlr_solve",
    )(right_sides, basis_u, basis_v, coupling)


def solution(mesh):
    in_specs = (
        P(("grp", "sub"), None),
        P(None, ("grp", "sub"), None),
        P(None, ("grp", "sub"), None),
        P(None, ("grp", "sub"), None),
    )
    out_specs = P(("grp", "sub"), None)
    return jax.shard_map(
        per_device, mesh=mesh, in_specs=in_specs, out_specs=out_specs, check_vma=False
    )
```

time: 293 us -> 71.7 us (0.24)
  the two profiles are of different devices: /device:TPU:194 before, /device:TPU:1 now
where the time goes in v2:
time: 71.7 us; the launch traced here: 71.5 us
  Pallas kernels  69.9 us (97%)
  local copies, waits for them, and re-layouts  1.67 us (2%)
    pallas_call x1, Pallas kernels, per_device(): pl.pallas_call(kernel, out_shape=jax.ShapeDtypeStruct((PTS, COLS), F32),...  69.9 us
    unnamed x1, local copies, waits for them, and re-layouts  1.67 us

profile of v2, /device:TPU:1, one launch (start us, length us, event | category | flops | bytes accessed | tf_op | source)
XLA Modules:
  0.0 71.5 jit_solution(16601936740810103058)
XLA Ops:
  0.0 69.9 %hodlr_solve.1 = f32[512,128]{1,0:T(8,128)} custom-call(f32[512,128]{1,0:T(8,128)} %rs_hbm.1, bf16[5,512,256]{2,1,0:T(8,128)(2,1)} %u_hbm.1, bf16[5,512,256]{2,1,0:T(8,128)(2,1)} %v_hbm.1, bf16[5,256,512]{2,1,0:T(8,128)(2,1)} %c_hbm.1), custom_call_target="tpu_custom_call" | custom-call | tf_op jit(solution)/shard_map/hodlr_solve/pallas_call | solution.py:328
  69.9 1.7 %copy.6 = f32[512,128]{1,0:T(8,128)} copy(f32[512,128]{1,0:T(8,128)} %hodlr_solve.1) | data formatting | bytes 524288

commit v3 on v2

--- a/solution.py
+++ b/solution.py
@@ -13,7 +13,7 @@
 PTS = 512
 COLS = 128
 LEVELS = 5
-SEMS = 32
+SEMS = 29
 SL = 8
 XS = 16
 
@@ -45,7 +45,7 @@
 def kernel(rs_hbm, u_hbm, v_hbm, c_hbm, out_ref, r0, u, v, cpl, cur_t,
            l0, rc0, r0s, lx, rcx, rxs, l1, rc1, r1s, lb, rcb, rbs,
            px, slb, zbr, ybr, x1, xb, x1h, x1l, xbh, xbl,
-           p0, q0r, p1, q1p, p2, q2p, q2s, p3, q3p, q3s, p4, q4p,
+           q0r, p1, q1p, p2, q2p, q2s, p3, q3p, q3s, p4, q4p,
            wall, ld, ss, rs):
     y = lax.axis_index("grp")
     s = lax.axis_index("sub")
@@ -56,10 +56,17 @@
     base = s - lane
 
     def near(k):
-        return (y, base + (lane + k) % 16)
+        c = (core + k % 2) % 2
+        return (y, base + 2 * chip_at(k // 2) + c)
+
+    def chip_at(k):
+        return 4 * ((chip // 4 + k % 2) % 2) + (chip % 4 + k // 2) % 4
 
     def same_core(k):
-        return (y, base + 2 * ((chip + k) % 8) + core)
+        return (y, base + 2 * chip_at(k) + core)
+
+    chips = (5, 4, 3, 7, 2, 6, 1)
+    devices = [2 * k + c for k in chips for c in (0, 1)] + [1]
 
     other_core = (y, s + 1 - 2 * core)
     plane_by = {1: plane + 1 - 2 * (plane % 2), 2: (plane + 2) % 4, 3: 3 - plane}
@@ -70,12 +77,15 @@
         ss_ = s + 16 * (plane_by[zmask] - plane) if zmask else s
         return (y_by[ymask] if ymask else y, ss_)
 
+    def hops(zmask, ymask):
+        return (0, 2, 4, 2)[zmask] + (0, 1, 2, 3, 4, 0, 2)[ymask]
+
     far_masks = [(1, 0), (2, 0), (3, 0), (0, 1), (1, 1), (2, 1), (3, 1), (0, 2), (0, 3), (0, 4), (0, 6)]
     MESH = pl.DeviceIdType.MESH
     barrier = pltpu.get_barrier_semaphore()
-    for m in far_masks:
+    for m in sorted(far_masks, key=lambda m: -hops(*m)):
         pl.semaphore_signal(barrier, inc=1, device_id=far(*m), device_id_type=MESH)
-    for k in range(1, 16):
+    for k in devices:
         pl.semaphore_signal(barrier, inc=1, device_id=near(k), device_id_type=MESH)
 
     loads = {}
@@ -84,11 +94,18 @@
         loads[name] = pltpu.make_async_copy(src, dst, ld.at[len(loads)])
         loads[name].start()
 
-    load("r", rs_hbm, r0)
-    for name in ("v0", "u0", "v1", "c0", "u2", "v3", "v4", "u3", "c1", "u1", "v2", "c2", "c3", "c4", "u4"):
-        src, dst = {"u": (u_hbm, u), "v": (v_hbm, v), "c": (c_hbm, cpl)}[name[0]]
-        load(name, src.at[int(name[1])], dst.at[int(name[1])])
-
+    def load_all(names):
+        for name in names:
+            load_one(name)
+
+    def load_one(name):
+        if name == "r":
+            load(name, rs_hbm, r0)
+        else:
+            src, dst = {"u": (u_hbm, u), "v": (v_hbm, v), "c": (c_hbm, cpl)}[name[0]]
+            load(name, src.at[int(name[1])], dst.at[int(name[1])])
+
+    load_all(("r", "v0", "v1", "u0"))
     pending = []
     count = [0]
 
@@ -126,7 +143,7 @@
         rc[...] = rc[...] + l[core]
 
     def rs_send(rc, slots):
-        return send([(rc.at[(chip + k) % 8], slots.at[k - 1], same_core(k)) for k in range(1, 8)], slots)
+        return send([(rc.at[chip_at(k)], slots.at[k - 1], same_core(k)) for k in chips], slots)
 
     def rs_sum(cp, rc, slots):
         cp.wait_recv()
@@ -137,7 +154,7 @@
 
     def ag_send(full, first=0, size=XS):
         own = full.at[core, chip, pl.ds(first, size)]
-        return send([(own, own, same_core(k)) for k in range(1, 8)], full.at[core, pl.ds(0, 7), pl.ds(first, size)])
+        return send([(own, own, same_core(k)) for k in chips], full.at[core, pl.ds(0, 7), pl.ds(first, size)])
 
     def share_send(cp, full, first=0, size=XS):
         cp.wait_recv()
@@ -146,12 +163,13 @@
                     full.at[1 - core, pl.ds(0, 8), rows])
 
     def all_send(src, slots, masks):
-        return send([(src, slots.at[i], far(*m)) for i, m in enumerate(masks)], slots)
+        order = sorted(range(len(masks)), key=lambda i: -hops(*masks[i]))
+        return send([(src, slots.at[i], far(*masks[i])) for i in order], slots)
 
     def w_send(level, value):
         mine = wall.at[level, core * 8 + chip]
         mine[...] = value
-        return send([(mine, mine, near(k)) for k in range(1, 16)], wall.at[level, pl.ds(0, 15)])
+        return send([(mine, mine, near(k)) for k in devices], wall.at[level, pl.ds(0, 15)])
 
     def w_full(level, cp):
         cp.wait_recv()
@@ -184,13 +202,14 @@
     cur_t[...] = rt
     rts = stacked(rt)
     loads["v0"].wait()
-    l0[...] = slices(halves(mm(rts, v[0])), SL)
+    l0[:, :, 0:SL, :] = slices(halves(mm(rts, v[0])), SL)
+    loads["v1"].wait()
+    l0[:, :, SL:2 * SL, :] = slices(halves(mm(rts, v[1])), SL)
     pl.semaphore_wait(barrier, len(far_masks) + 15)
     c_0 = core_send(l0, rc0)
-    loads["v1"].wait()
     loads["u0"].wait()
-    lx[:, :, 0:SL, :] = slices(halves(mm(rts, v[1])), SL)
-    lx[:, :, SL:SL + XS, :] = slices(mm(u[0].T, v[1]), XS)
+    load_all(("u2", "v3", "v4", "u3", "c0", "u1", "v2", "c1", "c2", "c3", "c4", "u4"))
+    lx[...] = slices(mm(u[0].T, v[1]), XS)
     c_x = core_send(lx, rcx)
     core_add(c_0, l0, rc0)
     g_0 = rs_send(rc0, r0s)
@@ -206,21 +225,20 @@
     ut = u[3].T
     lb[:, :, 2 * XS:3 * XS, :] = slices(mm(ut, v[4]), XS)
     c_b = core_send(lb, rcb)
-    p0[...] = rs_sum(g_0, rc0, r0s)
-    e_0 = all_send(p0, q0r, [(1, 0)])
-    px[...] = rs_sum(g_x, rcx, rxs)
-    x1[core, chip] = px[SL:SL + XS]
+    px[...] = rs_sum(g_0, rc0, r0s)
+    e_0 = all_send(px.at[pl.ds(0, SL)], q0r, [(1, 0)])
+    x1[core, chip] = rs_sum(g_x, rcx, rxs)
     a_x = ag_send(x1)
     core_add(c_b, lb, rcb)
     e_0.wait_recv()
-    w_0 = weights(0, p0[...], q0r[0], bit4)
+    w_0 = weights(0, px[0:SL], q0r[0], bit4)
     ws = stacked(w_0)
     w_cps[0] = w_send(0, w_0)
     g_b = rs_send(rcb, rbs)
     s_x = share_send(a_x, x1)
     s_x.wait_recv()
     split_full(x1, x1h, x1l, 0, 1)
-    p1[...] = px[0:SL] - product(ws, x1h[0], x1l[0])
+    p1[...] = px[SL:2 * SL] - product(ws, x1h[0], x1l[0])
     e_1 = all_send(p1, q1p, planes)
     w0 = w_full(0, w_cps[0])
     cur_t[...] = cur_t[...] - halves(mm_t(w0, u[0]))
@@ -309,15 +327,15 @@
         vm(PTS, COLS), vm(LEVELS, PTS, RANK, dtype=BF16), vm(LEVELS, PTS, RANK, dtype=BF16),
         vm(LEVELS, RANK, 2 * RANK, dtype=BF16), vm(COLS, PTS),
     ]
-    for n in (SL, SL + XS, 3 * SL, 3 * XS):
+    for n in (2 * SL, XS, 3 * SL, 3 * XS):
         scratch += [vm(2, 8, n, RANK), vm(8, n, RANK), vm(7, n, RANK)]
     scratch += [
-        vm(SL + XS, RANK), vm(3 * XS, RANK), vm(3, 3 * XS, RANK), vm(1, XS, RANK),
+        vm(2 * SL, RANK), vm(3 * XS, RANK), vm(3, 3 * XS, RANK), vm(1, XS, RANK),
         vm(2, 8, XS, RANK), vm(2, 8, 3 * XS, RANK),
     ]
     scratch += [vm(1, RANK, RANK, dtype=BF16)] * 2 + [vm(3, RANK, RANK, dtype=BF16)] * 2
     scratch += [
-        vm(SL, RANK), vm(1, SL, RANK),
+        vm(1, SL, RANK),
         vm(SL, RANK), vm(3, SL, RANK),
         vm(3 * SL, RANK), vm(7, SL, RANK), vm(3, 2 * SL, RANK),
         vm(2 * SL, RANK), vm(3, SL, RANK), vm(1, SL, RANK),
@@ -331,7 +349,7 @@
         in_specs=[pl.BlockSpec(memory_space=pltpu.HBM)] * 4,
         out_specs=pl.BlockSpec(memory_space=pltpu.VMEM),
         scratch_shapes=scratch,
-        compiler_params=pltpu.CompilerParams(collective_id=0, has_side_effects=True, vmem_limit_bytes=60 * 2**20),
+        compiler_params=pltpu.CompilerParams(collective_id=0, has_side_effects=True, vmem_limit_bytes=int(53.5 * 2**20)),
         name="hodlr_solve",
     )(right_sides, basis_u, basis_v, coupling)
 

time: 71.7 us -> 69 us (0.962)
  Pallas kernels: 69.9 us -> 68.1 us
  local copies, waits for them, and re-layouts: 1.67 us -> 0.71 us
    pallas_call x1, Pallas kernels: 69.9 us -> 68.1 us  [per_device(): pl.pallas_call(kernel, out_shape=jax.ShapeDtypeStruct((PTS, COLS), F32),...]
    unnamed x1, local copies, waits for them, and re-layouts: 1.67 us -> 0.71 us
where the time goes in v3:
time: 69 us; the launch traced here: 68.9 us
  Pallas kernels  68.1 us (99%)
  local copies, waits for them, and re-layouts  0.71 us (1%)
    pallas_call x1, Pallas kernels, per_device(): pl.pallas_call(kernel, out_shape=jax.ShapeDtypeStruct((PTS, COLS), F32),...  68.1 us

profile of v3, /device:TPU:1, one launch (start us, length us, event | category | flops | bytes accessed | tf_op | source)
XLA Modules:
  0.0 68.9 jit_solution(9693411012415810969)
XLA Ops:
  0.0 68.1 %hodlr_solve.1 = f32[512,128]{1,0:T(8,128)S(1)} custom-call(f32[512,128]{1,0:T(8,128)} %rs_hbm.1, bf16[5,512,256]{2,1,0:T(8,128)(2,1)} %u_hbm.1, bf16[5,512,256]{2,1,0:T(8,128)(2,1)} %v_hbm.1, bf16[5,256,512]{2,1,0:T(8,128)(2,1)} %c_hbm.1), custom_call_target="tpu_custom_call" | custom-call | tf_op jit(solution)/shard_map/hodlr_solve/pallas_call | solution.py:346
  68.1 0.7 %copy.6 = f32[512,128]{1,0:T(8,128)} copy(f32[512,128]{1,0:T(8,128)S(1)} %hodlr_solve.1) | data formatting | bytes 524288

commit v4 on v3

--- a/solution.py
+++ b/solution.py
@@ -13,7 +13,7 @@
 PTS = 512
 COLS = 128
 LEVELS = 5
-SEMS = 29
+SEMS = 30
 SL = 8
 XS = 16
 
@@ -43,10 +43,10 @@
 
 
 def kernel(rs_hbm, u_hbm, v_hbm, c_hbm, out_ref, r0, u, v, cpl, cur_t,
-           l0, rc0, r0s, lx, rcx, rxs, l1, rc1, r1s, lb, rcb, rbs,
+           l0, rc0, r0s, lx, rcx, rxs, l1, rc1, r1s, l2, rc2, r2s, lb, rcb, rbs,
            px, slb, zbr, ybr, x1, xb, x1h, x1l, xbh, xbl,
            q0r, p1, q1p, p2, q2p, q2s, p3, q3p, q3s, p4, q4p,
-           wall, ld, ss, rs):
+           wall, wpair, ld, ss, rs):
     y = lax.axis_index("grp")
     s = lax.axis_index("sub")
     core = s % 2
@@ -77,6 +77,12 @@
         ss_ = s + 16 * (plane_by[zmask] - plane) if zmask else s
         return (y_by[ymask] if ymask else y, ss_)
 
+    def far_other(zmask, ymask):
+        y_, s_ = far(zmask, ymask)
+        return (y_, s_ + 1 - 2 * core)
+
+    both = [(1, 0), (2, 0), (3, 0), (0, 2), (0, 4), (0, 6)]
+
     def hops(zmask, ymask):
         return (0, 2, 4, 2)[zmask] + (0, 1, 2, 3, 4, 0, 2)[ymask]
 
@@ -85,6 +91,8 @@
     barrier = pltpu.get_barrier_semaphore()
     for m in sorted(far_masks, key=lambda m: -hops(*m)):
         pl.semaphore_signal(barrier, inc=1, device_id=far(*m), device_id_type=MESH)
+    for m in both:
+        pl.semaphore_signal(barrier, inc=1, device_id=far_other(*m), device_id_type=MESH)
     for k in devices:
         pl.semaphore_signal(barrier, inc=1, device_id=near(k), device_id_type=MESH)
 
@@ -171,8 +179,27 @@
         mine[...] = value
         return send([(mine, mine, near(k)) for k in devices], wall.at[level, pl.ds(0, 15)])
 
+    def pair_send(src, slots, masks):
+        slots[4 * core] = src[...]
+        order = sorted(range(len(masks)), key=lambda i: -hops(*masks[i]))
+        copies = [(src, slots.at[4 * core + 1 + i], to(*masks[i])) for i in order for to in (far, far_other)]
+        return send(copies + [(src, slots.at[4 * core], other_core)], slots.at[pl.ds(0, 7)])
+
+    def pair_weights(level, q, upper):
+        own = jnp.concatenate([q[0] + q[1], q[4] + q[5]], axis=0)
+        sibling = jnp.concatenate([q[2] + q[3], q[6] + q[7]], axis=0)
+        return weights(level, own, sibling, upper)
+
+    def pair_w_send(i, value):
+        wpair[i, 0, chip] = value[:SL]
+        wpair[i, 1, chip] = value[SL:]
+        mine = wpair.at[i, pl.ds(0, 2), chip]
+        return send([(mine, mine, same_core(k)) for k in chips], wpair.at[i, pl.ds(0, 2), pl.ds(0, 7)])
+
     def w_full(level, cp):
         cp.wait_recv()
+        if level in (1, 4):
+            return stacked(wpair[level // 4].reshape(COLS, RANK))
         return stacked(wall[level].reshape(COLS, RANK))
 
     def weights(level, own, sibling, upper):
@@ -205,7 +232,7 @@
     l0[:, :, 0:SL, :] = slices(halves(mm(rts, v[0])), SL)
     loads["v1"].wait()
     l0[:, :, SL:2 * SL, :] = slices(halves(mm(rts, v[1])), SL)
-    pl.semaphore_wait(barrier, len(far_masks) + 15)
+    pl.semaphore_wait(barrier, len(far_masks) + len(both) + 15)
     c_0 = core_send(l0, rc0)
     loads["u0"].wait()
     load_all(("u2", "v3", "v4", "u3", "c0", "u1", "v2", "c1", "c2", "c3", "c4", "u4"))
@@ -239,7 +266,7 @@
     s_x.wait_recv()
     split_full(x1, x1h, x1l, 0, 1)
     p1[...] = px[SL:2 * SL] - product(ws, x1h[0], x1l[0])
-    e_1 = all_send(p1, q1p, planes)
+    e_1 = pair_send(p1, q1p, planes)
     w0 = w_full(0, w_cps[0])
     cur_t[...] = cur_t[...] - halves(mm_t(w0, u[0]))
     upd = mm_t(u[0], w0)
@@ -257,24 +284,29 @@
     z_b = all_send(slb, zbr, planes)
 
     e_1.wait_recv()
-    w_cps[1] = w_send(1, weights(1, p1[...] + q1p[0], q1p[1] + q1p[2], bit5))
+    w_cps[1] = pair_w_send(0, pair_weights(1, q1p, bit5))
 
     loads["u1"].wait()
     loads["v2"].wait()
     w1 = w_full(1, w_cps[1])
     cur_s = stacked(cur_t[...] - halves(mm_t(w1, u[1])))
-    for m in (2, 3, 4):
-        l1[:, :, (m - 2) * SL:(m - 1) * SL, :] = slices(halves(mm(cur_s, v[m])), SL)
+    l1[...] = slices(halves(mm(cur_s, v[2])), SL)
     c_1 = core_send(l1, rc1)
+    for m in (3, 4):
+        l2[:, :, (m - 3) * SL:(m - 2) * SL, :] = slices(halves(mm(cur_s, v[m])), SL)
+    c_2 = core_send(l2, rc2)
     core_add(c_1, l1, rc1)
     g_1 = rs_send(rc1, r1s)
+    core_add(c_2, l2, rc2)
+    g_2 = rs_send(rc2, r2s)
     z_b.wait_recv()
     xb[core, chip] = slb[...] + zbr[0] + (zbr[1] + zbr[2])
     y_b = all_send(xb.at[core, chip, pl.ds(2 * XS, XS)], ybr, [(0, 1)])
     a_b = ag_send(xb, 0, 2 * XS)
-    p2[...] = rs_sum(g_1, rc1, r1s)
+    p2[0:SL] = rs_sum(g_1, rc1, r1s)
     peers = [(1, 0), (2, 0), (3, 0), (0, 1), (1, 1), (2, 1), (3, 1)]
     e_2 = all_send(p2.at[pl.ds(0, SL)], q2p, peers)
+    p2[SL:3 * SL] = rs_sum(g_2, rc2, r2s)
     e_2s = all_send(p2.at[pl.ds(SL, 2 * SL)], q2s, planes)
     flush_old()
     y_b.wait_recv()
@@ -307,14 +339,13 @@
     w = weights(3, p3[0:SL] + q3p[0], q3p[1] + q3p[2], (y // 2) % 2)
     e_3s.wait_recv()
     p4[...] = p3[SL:2 * SL] + q3s[0] - product(stacked(w), xbh[2], xbl[2])
-    e_4 = all_send(p4, q4p, [(0, 2), (0, 4), (0, 6)])
+    e_4 = pair_send(p4, q4p, [(0, 2), (0, 4), (0, 6)])
     flush_old()
     w_cps[3] = w_send(3, w)
     apply(3)
 
     e_4.wait_recv()
-    w = weights(4, p4[...] + q4p[0], q4p[1] + q4p[2], y // 4)
-    w_cps[4] = w_send(4, w)
+    w_cps[4] = pair_w_send(1, pair_weights(4, q4p, y // 4))
     apply(4)
     flush()
 
@@ -327,7 +358,7 @@
         vm(PTS, COLS), vm(LEVELS, PTS, RANK, dtype=BF16), vm(LEVELS, PTS, RANK, dtype=BF16),
         vm(LEVELS, RANK, 2 * RANK, dtype=BF16), vm(COLS, PTS),
     ]
-    for n in (2 * SL, XS, 3 * SL, 3 * XS):
+    for n in (2 * SL, XS, SL, 2 * SL, 3 * XS):
         scratch += [vm(2, 8, n, RANK), vm(8, n, RANK), vm(7, n, RANK)]
     scratch += [
         vm(2 * SL, RANK), vm(3 * XS, RANK), vm(3, 3 * XS, RANK), vm(1, XS, RANK),
@@ -336,11 +367,11 @@
     scratch += [vm(1, RANK, RANK, dtype=BF16)] * 2 + [vm(3, RANK, RANK, dtype=BF16)] * 2
     scratch += [
         vm(1, SL, RANK),
-        vm(SL, RANK), vm(3, SL, RANK),
+        vm(SL, RANK), vm(8, SL, RANK),
         vm(3 * SL, RANK), vm(7, SL, RANK), vm(3, 2 * SL, RANK),
         vm(2 * SL, RANK), vm(3, SL, RANK), vm(1, SL, RANK),
-        vm(SL, RANK), vm(3, SL, RANK),
-        vm(LEVELS, 16, SL, RANK),
+        vm(SL, RANK), vm(8, SL, RANK),
+        vm(LEVELS, 16, SL, RANK), vm(2, 2, 8, SL, RANK),
         pltpu.SemaphoreType.DMA((16,)), pltpu.SemaphoreType.DMA((SEMS,)), pltpu.SemaphoreType.DMA((SEMS,)),
     ]
     return pl.pallas_call(

time: 69 us -> 67.1 us (0.972)
  Pallas kernels: 68.1 us -> 66 us
    pallas_call x1, Pallas kernels: 68.1 us -> 66 us  [per_device(): pl.pallas_call(kernel, out_shape=jax.ShapeDtypeStruct((PTS, COLS), F32),...]
where the time goes in v4:
time: 67.1 us; the launch traced here: 66.7 us
  Pallas kernels  66 us (98%)
  local copies, waits for them, and re-layouts  0.71 us (1%)
    pallas_call x1, Pallas kernels, per_device(): pl.pallas_call(kernel, out_shape=jax.ShapeDtypeStruct((PTS, COLS), F32),...  66 us

profile of v4, /device:TPU:1, one launch (start us, length us, event | category | flops | bytes accessed | tf_op | source)
XLA Modules:
  0.0 66.7 jit_solution(8342131030615662343)
XLA Ops:
  0.0 66.0 %hodlr_solve.1 = f32[512,128]{1,0:T(8,128)S(1)} custom-call(f32[512,128]{1,0:T(8,128)} %rs_hbm.1, bf16[5,512,256]{2,1,0:T(8,128)(2,1)} %u_hbm.1, bf16[5,512,256]{2,1,0:T(8,128)(2,1)} %v_hbm.1, bf16[5,256,512]{2,1,0:T(8,128)(2,1)} %c_hbm.1), custom_call_target="tpu_custom_call" | custom-call | tf_op jit(solution)/shard_map/hodlr_solve/pallas_call | solution.py:377
  66.0 0.7 %copy.6 = f32[512,128]{1,0:T(8,128)} copy(f32[512,128]{1,0:T(8,128)S(1)} %hodlr_solve.1) | data formatting | bytes 524288

commit v5 on v4

--- a/solution.py
+++ b/solution.py
@@ -257,11 +257,11 @@
     x1[core, chip] = rs_sum(g_x, rcx, rxs)
     a_x = ag_send(x1)
     core_add(c_b, lb, rcb)
+    g_b = rs_send(rcb, rbs)
     e_0.wait_recv()
     w_0 = weights(0, px[0:SL], q0r[0], bit4)
     ws = stacked(w_0)
     w_cps[0] = w_send(0, w_0)
-    g_b = rs_send(rcb, rbs)
     s_x = share_send(a_x, x1)
     s_x.wait_recv()
     split_full(x1, x1h, x1l, 0, 1)

time: 67.1 us -> 68.6 us (1.022)
  Pallas kernels: 66 us -> 67.7 us
    pallas_call x1, Pallas kernels: 66 us -> 67.7 us  [per_device(): pl.pallas_call(kernel, out_shape=jax.ShapeDtypeStruct((PTS, COLS), F32),...]
where the time goes in v5:
time: 68.6 us; the launch traced here: 68.5 us
  Pallas kernels  67.7 us (99%)
  local copies, waits for them, and re-layouts  0.71 us (1%)
    pallas_call x1, Pallas kernels, per_device(): pl.pallas_call(kernel, out_shape=jax.ShapeDtypeStruct((PTS, COLS), F32),...  67.7 us

profile of v5, /device:TPU:1, one launch (start us, length us, event | category | flops | bytes accessed | tf_op | source)
XLA Modules:
  0.0 68.5 jit_solution(16562024359686570774)
XLA Ops:
  0.0 67.7 %hodlr_solve.1 = f32[512,128]{1,0:T(8,128)S(1)} custom-call(f32[512,128]{1,0:T(8,128)} %rs_hbm.1, bf16[5,512,256]{2,1,0:T(8,128)(2,1)} %u_hbm.1, bf16[5,512,256]{2,1,0:T(8,128)(2,1)} %v_hbm.1, bf16[5,256,512]{2,1,0:T(8,128)(2,1)} %c_hbm.1), custom_call_target="tpu_custom_call" | custom-call | tf_op jit(solution)/shard_map/hodlr_solve/pallas_call | solution.py:377
  67.7 0.7 %copy.6 = f32[512,128]{1,0:T(8,128)} copy(f32[512,128]{1,0:T(8,128)S(1)} %hodlr_solve.1) | data formatting | bytes 524288
